TPU v7x, 1024 devices: a whole 8x8x8 slice. The times are simulated.
1024 devices in a mesh: expert: 64 (over z, x), tensor: 16 (over y, core).
Axes of the slice: x: 8, y: 8, z: 8, core: 2. Of those that a mesh axis runs over, the one named last changes fastest.
Arguments:
- routes: int32 [3072, 8], P('expert'), may hold values from 0 to 63, all different within a row; in each aligned block of 48 rows (0 to 47, 48 to 95, ...) at most 9 rows name the same one
- gates: float32 [3072, 8], P('expert'), may hold values from 0.05 to 0.4
- hidden: bfloat16 [64, 576, 3072], P('expert', None, 'tensor'), may hold values from -6 to 6
- down: bfloat16 [64, 3072, 4096], P('expert', None, 'tensor'), may hold values from -0.109375 to 0.109375
- out_grad: bfloat16 [3072, 4096], P('expert', 'tensor'), may hold values from -6 to 6
Outputs:
- mixed: bfloat16 [3072, 4096], P('expert', 'tensor')
- hidden_grad: bfloat16 [64, 576, 3072], P('expert', None, 'tensor')
Inputs may be any that keep to these rules, and one draw needn't show every extreme that they name: `routes`: each row names 8 different experts. Within the rows of one token block (48 rows, aligned), no expert is named more than 9 times, a bound that some block reaches.
All inputs are finite; a program needn't handle non-finite values.
Results may differ from a plain program's by a relative error of at most 0.0049.
Values may be sent and summed in bfloat16 or wider, within the bound.
A program may use at most 32 MiB of HBM per device.

v0:
```python
import jax
import jax.numpy as jnp
from jax import lax
from jax.sharding import PartitionSpec as P


def slot_numbers(block_routes, count):
    flat_index = block_routes.reshape(-1)
    onehot = (flat_index[:, None] == jnp.arange(count, dtype=jnp.int32)[None, :]).astype(jnp.int32)
    before = jnp.cumsum(onehot, axis=0) - onehot
    return jnp.sum(before * onehot, axis=1).reshape(block_routes.shape)


def body(routes, gates, hidden, down, out_grad):
    experts = lax.axis_size("expert")
    slot_rows = hidden.shape[1]
    capacity = slot_rows // experts
    tok_rows = routes.shape[0]
    top_count = routes.shape[1]
    feat_local = out_grad.shape[1]
    weights = down[0]
    slot = slot_numbers(routes, experts)
    flat_index = (routes * capacity + slot).reshape(-1)
    scaled = (gates[:, :, None] * out_grad.astype(jnp.float32)[:, None, :]).astype(jnp.bfloat16)
    outgoing = (
        jnp.zeros((slot_rows, feat_local), jnp.bfloat16)
        .at[flat_index]
        .set(scaled.reshape(tok_rows * top_count, feat_local))
    )
    outgoing = outgoing.reshape(experts, capacity, feat_local)
    arrived = lax.all_to_all(outgoing, "expert", split_axis=0, concat_axis=0, tiled=True)
    summed = jnp.dot(
        lax.all_gather(hidden[0], "tensor", axis=1, tiled=True),
        weights,
        preferred_element_type=jnp.float32,
    )
    expert_out = summed.astype(jnp.bfloat16).reshape(experts, capacity, feat_local)
    returned = lax.all_to_all(expert_out, "expert", split_axis=0, concat_axis=0, tiled=True)
    gathered_out = returned.reshape(slot_rows, feat_local)[flat_index].reshape(
        tok_rows, top_count, feat_local
    )
    mixed = jnp.sum(gates[:, :, None] * gathered_out.astype(jnp.float32), axis=1).astype(
        jnp.bfloat16
    )
    arrived_rows = arrived.reshape(slot_rows, feat_local)
    partial_value = lax.dot_general(
        arrived_rows, weights, (((1,), (1,)), ((), ())), preferred_element_type=jnp.float32
    )
    grad_hidden = lax.psum_scatter(partial_value, "tensor", scatter_dimension=1, tiled=True)
    return (mixed, grad_hidden.astype(jnp.bfloat16)[None])


def solution(mesh):
    return jax.shard_map(
        body,
        mesh=mesh,
        in_specs=(
            P("expert", None),
            P("expert", None),
            P("expert", None, "tensor"),
            P("expert", None, "tensor"),
            P("expert", "tensor"),
        ),
        out_specs=(P("expert", "tensor"), P("expert", None, "tensor")),
        check_vma=False,
    )
```

profile of v0, /device:TPU:1, one launch (start us, length us, event | category | flops | bytes accessed | tf_op | source)
XLA Modules:
  0.0 155.5 jit_solution(17513304372206963032)
XLA Ops:
  7.2 0.0 all-gather.3.cloned.1.call-start
  7.2 0.7 all-gather.3.cloned.1.call-update
  7.9 0.0 reduce-scatter.2.cloned.1.call-start
  8.0 0.8 copy.16
  8.7 0.1 eq.29
  8.8 0.1 eq.25
  8.9 0.8 copy.15
  9.7 0.1 mul.40
  9.8 0.7 convert_element_type.35
  10.5 0.9 reduce-window.6
  11.4 0.2 slice_reduce_fusion
  11.7 0.1 fusion.19
  11.8 0.1 reshape.78
  11.9 0.1 copy.19
  12.0 0.7 multiply_add_fusion
  12.7 0.1 copy.20
  12.8 0.1 reshape.79
  12.9 2.1 %scatter_custom_fusion = bf16[576,256]{1,0:T(8,128)(2,1)S(1)} fusion(s32[384]{0:T(512)S(1)} %fusion.21, f32[48,256]{1,0:T(8,128)S(1)} %convert_element_type.35, f32[384]{0:T(512)S(1)} %mul.40, bf16[]{:T(256)} %constant.14.clone.1), kind=kCustom, calls=%fused_computation.13 | custom fusion | flops 196608 | bytes 346114 | tf_op jit(solution)/shard_map/scatter | solution.py:28
  15.0 0.1 reshape.80
  15.1 40.1 %all_to_all.10 = bf16[64,9,256]{2,1,0:T(8,128)(2,1)S(1)} all-to-all(bf16[64,9,256]{2,1,0:T(8,128)(2,1)S(1)} %reshape.80), channel_id=1, replica_groups=mesh['expert'=64,'tensor'=16] {'expert'}, dimensions={0} | all-to-all | bytes 589824 | tf_op jit(solution)/shard_map/all_to_all | solution.py:31
  55.2 0.1 reshape.81
  55.4 4.5 %fusion.2 = f32[576,3072]{0,1:T(8,128)} fusion(bf16[576,256]{1,0:T(8,128)(2,1)S(1)} %reshape.81, bf16[1,3072,256]{2,1,0:T(8,128)(2,1)S(1)} %copy-done), kind=kOutput, calls=%fused_computation.4 | convolution fusion | flops 905969664 | bytes 8945664 | tf_op jit(solution)/shard_map/dot_general | solution.py:46
  59.9 10.5 %all-gather.3.cloned.1.call-done = bf16[1,576,3072]{1,2,0:T(8,128)(2,1)} async-done(((bf16[1,576,192]{1,2,0:T(8,128)(2,1)}), bf16[1,576,3072]{1,2,0:T(8,128)(2,1)}) %all-gather.3.cloned.1.call-update) | async-done | bytes 3538960 | tf_op jit(solution)/shard_map/all_gather | solution.py:33
  70.4 3.5 %fusion.5 = bf16[576,256]{1,0:T(8,128)(2,1)S(1)} fusion(bf16[1,3072,256]{2,1,0:T(8,128)(2,1)S(1)} %copy-done, bf16[1,576,3072]{1,2,0:T(8,128)(2,1)} %all-gather.3.cloned.1.call-done), kind=kOutput, calls=%fused_computation.7 | convolution fusion | flops 906117120 | bytes 5406720 | tf_op jit(solution)/shard_map/dot_general | solution.py:32
  73.8 0.9 reshape.75
  74.8 13.8 %all-to-all-start = ((bf16[64,9,256]{2,1,0:T(8,128)(2,1)}), bf16[64,9,256]{2,1,0:T(8,128)(2,1)S(1)}, u32[]{:S(2)}, u32[]{:S(2)}) async-start(bf16[64,9,256]{2,1,0:T(8,128)(2,1)} %reshape.75), calls=%async_computation | async-start | bytes 1048576 | tf_op jit(solution)/shard_map/all_to_all | solution.py:38
  88.6 17.8 %all-to-all-done = bf16[64,9,256]{2,1,0:T(8,128)(2,1)S(1)} async-done(((bf16[64,9,256]{2,1,0:T(8,128)(2,1)}), bf16[64,9,256]{2,1,0:T(8,128)(2,1)S(1)}, u32[]{:S(2)}, u32[]{:S(2)}) %all-to-all-start) | async-done | bytes 294944 | tf_op jit(solution)/shard_map/all_to_all | solution.py:38
  106.4 0.1 reshape.76
  106.6 2.1 %gather_fusion = bf16[384,256]{1,0:T(8,128)(2,1)S(1)} fusion(bf16[576,256]{1,0:T(8,128)(2,1)S(1)} %reshape.76, s32[1024]{0:T(1024)S(1)} %pad_clamp_fusion), kind=kCustom, calls=%fused_computation | custom fusion | bytes 394752 | tf_op jit(solution)/shard_map/gather | solution.py:39
  108.6 0.8 fusion.10
  109.4 37.5 %reduce-scatter.2.cloned.1.call-done = f32[576,192]{0,1:T(8,128)} async-done(((f32[576,3072]{0,1:T(8,128)}), f32[576,192]{0,1:T(8,128)}) %reduce-scatter.2.cloned.1.call-update) | async-done | bytes 442384 | tf_op jit(solution)/shard_map/reduce_scatter | solution.py:49
  146.9 1.8 %convert_bitcast_fusion = bf16[1,576,192]{1,2,0:T(8,128)(2,1)} fusion(f32[576,192]{0,1:T(8,128)} %reduce-scatter.2.cloned.1.call-done), kind=kLoop, calls=%fused_computation.12 | loop fusion | flops 110592 | bytes 663552 | tf_op jit(solution)/shard_map/broadcast_in_dim | solution.py:50
  (7 shorter events, 0.1 us)
Async XLA Ops:
  7.2 48.2 %copy-start = (bf16[1,3072,256]{2,1,0:T(8,128)(2,1)S(1)}, bf16[1,3072,256]{2,1,0:T(8,128)(2,1)}, u32[]{:S(2)}) copy-start(bf16[1,3072,256]{2,1,0:T(8,128)(2,1)} %param.8) | copy-start | bytes 4718596
  7.2 63.2 %all-gather.3.cloned.1.call-start = ((), (), s32[]{:S(2)}) async-start(), calls=%async_computation.4 | async-start | bytes 4177920 | tf_op jit(solution)/shard_map/all_gather | solution.py:33
  7.9 139.0 %reduce-scatter.2.cloned.1.call-start = ((), (), s32[]{:S(2)}) async-start(), calls=%async_computation.3 | async-start | bytes 8355840 | tf_op jit(solution)/shard_map/reduce_scatter | solution.py:49
  74.8 31.6 %all-to-all-start = ((bf16[64,9,256]{2,1,0:T(8,128)(2,1)}), bf16[64,9,256]{2,1,0:T(8,128)(2,1)S(1)}, u32[]{:S(2)}, u32[]{:S(2)}) async-start(bf16[64,9,256]{2,1,0:T(8,128)(2,1)} %reshape.75), calls=%async_computation | async-start | bytes 1048576 | tf_op jit(solution)/shard_map/all_to_all | solution.py:38
Sparse Core Ops, SparseCore 0:
  10.7 59.6 all-gather.2
  73.8 73.0 reduce-scatter.1
where the time goes:
time: 156 us; the launch traced here: 155 us
  waiting for transfers between devices  66.5 us (43%)
  blocking collectives  40.1 us (26%)
  between operations  14.1 us (9%)
  starting transfers between devices  13.9 us (9%)
  matrix products  7.97 us (5%)
  other arithmetic  7.17 us (5%)
  local copies, waits for them, and re-layouts  5.74 us (4%)
    all_to_all x1, blocking collectives, body(): lax.all_to_all(outgoing, 'expert', split_axis=0, concat_axis=0, tiled=True)  40.1 us
    reduce_scatter x1, waiting for transfers between devices, body(): lax.psum_scatter(partial_value, 'tensor', scatter_dimension=1, tiled=True)  37.5 us
    all_to_all x1, waiting for transfers between devices, body(): lax.all_to_all(expert_out, 'expert', split_axis=0, concat_axis=0, tiled=T...  17.8 us
    all_to_all x1, starting transfers between devices, body(): lax.all_to_all(expert_out, 'expert', split_axis=0, concat_axis=0, tiled=T...  13.8 us
    all_gather x1, waiting for transfers between devices, body(): lax.all_gather(hidden[0], 'tensor', axis=1, tiled=True)  10.5 us
    dot_general x1, matrix products, body(): lax.dot_general(arrived_rows, weights, (((1,), (1,)), ((), ())), preferre...  4.51 us
    dot_general x1, matrix products, body(): jnp.dot(lax.all_gather(hidden[0], 'tensor', axis=1, tiled=True), weights,...  3.46 us
  transfers between devices with their start and end apart: 3, of which 3 were waited for; matrix products, arithmetic and copies ran while one was open for 12% of the time, Pallas kernels for 0%

commit v1 on v0

v1 whole, which is shorter than its diff:
```python
import functools

import jax
import jax.numpy as jnp
from jax import lax
from jax.experimental import pallas as pl
from jax.experimental.pallas import tpu as pltpu
from jax.sharding import PartitionSpec as P

MESH = pl.DeviceIdType.MESH
GROUP = 16
BF, F32 = jnp.bfloat16, jnp.float32


def dot(a, b):
    return jnp.dot(a, b, preferred_element_type=F32)


def dot_nt(a, b):
    return lax.dot_general(a, b, (((1,), (1,)), ((), ())), preferred_element_type=F32)


def iota(shape, axis):
    return lax.broadcasted_iota(jnp.int32, shape, axis)


def kernel(
    sizes,
    routes_ref, gates_ref, grad_ref, hidden_ref, down_ref,
    mixed_ref, hgrad_ref,
    hin, wext, ring, acc_own, acc_sib, sib_in, rg,
    part, rs_out, rs_in, send_g, recv_g, send_e, recv_e,
    local_sem, ag_send, ag_recv, rs_send, rs_recv, sib_send, sib_recv, a2a_send, a2a_recv,
):
    ne, ny, cap, tok, top, rows, cols, feat = sizes
    half, quarter = rows // 2, rows // 4
    wide = 2 * cols
    pad = 256 - cols
    span = ne * GROUP
    me = lax.axis_index("expert")
    tt = lax.axis_index("tensor")
    y, core = tt // 2, tt % 2
    right = ((y + 1) % ny) * 2 + core
    left = ((y + ny - 1) % ny) * 2 + core
    other = y * 2 + (1 - core)

    copy_h = pltpu.make_async_copy(hidden_ref, hin, local_sem.at[0])
    copy_w = pltpu.make_async_copy(
        down_ref.at[:, core], wext.at[:, pl.ds(pad, cols), pl.ds(0, feat)], local_sem.at[1]
    )
    copy_h.start()
    copy_w.start()

    barrier = pltpu.get_barrier_semaphore()

    def greet(i, carry):
        pl.semaphore_signal(barrier, inc=1, device_id=((me + i) % ne, tt), device_id_type=MESH)
        return carry

    for peer in (right, left, other):
        pl.semaphore_signal(barrier, inc=1, device_id=(me, peer), device_id_type=MESH)
    lax.fori_loop(1, ne, greet, 0)

    wext[:, 0:pad, :] = jnp.zeros((ny, pad, 2 * feat), BF)
    wext[:, pad + cols :, :] = jnp.zeros((ny, pad, 2 * feat), BF)

    copy_h.wait()
    ring[0, :, 0:cols] = hin[0:half, :]
    ring[0, :, cols:wide] = hin[half:rows, :]

    pl.semaphore_wait(barrier, ne - 1 + 3)

    def remote(src, dst, send, recv, peer):
        return pltpu.make_async_remote_copy(
            src_ref=src, dst_ref=dst, send_sem=send, recv_sem=recv, device_id=(me, peer), device_id_type=MESH
        )

    copy_ws = remote(
        down_ref.at[:, 1 - core],
        wext.at[:, pl.ds(pad, cols), pl.ds(feat, feat)],
        sib_send.at[0],
        sib_recv.at[0],
        other,
    )
    copy_ws.start()

    def ag_place(way, i):
        step, which = i // 2, (i % 2) ^ way
        src, dst = (step, step + 1) if way == 0 else ((ny - step) % ny, ny - 1 - step)
        return src, dst, which

    ag = []
    for way in range(2):
        ag.append([])
        for i in range(ny - 1):
            src, dst, which = ag_place(way, i)
            chunk = pl.ds(which * quarter, quarter)
            ag[way].append(
                remote(ring.at[src, chunk], ring.at[dst, chunk], ag_send.at[way, i], ag_recv.at[way, i], (right, left)[way])
            )
    for i in range(2):
        for way in range(2):
            ag[way][i].start()

    with jax.named_scope("routing"):
        named = jnp.zeros((tok, ne), F32)
        gate = jnp.zeros((tok, ne), F32)
        for k in range(top):
            hit = routes_ref[:, k : k + 1] == iota((tok, ne), 1)
            named = named + jnp.where(hit, 1.0, 0.0)
            gate = gate + jnp.where(hit, gates_ref[:, k : k + 1], 0.0)
        earlier = jnp.where(iota((tok, tok), 1) < iota((tok, tok), 0), 1.0, 0.0).astype(BF)
        slot = jnp.where(named > 0.5, dot(earlier, named.astype(BF)), 100.0).astype(BF)
        gate_1 = gate.astype(BF)
        gate_2 = (gate - gate_1.astype(F32)).astype(BF)
        gate_3 = (gate - gate_1.astype(F32) - gate_2.astype(F32)).astype(BF)
        gate_of = (gate_1, gate_2, gate_3)

        spread = jnp.where(iota((span, ne), 0) // GROUP == iota((span, ne), 1), 1.0, 0.0).astype(BF)
        place = (iota((span, tok), 0) % GROUP).astype(F32)
        takes = dot_nt(spread, slot) == place
        gate_rows = dot_nt(spread, gate_1) + dot_nt(spread, gate_2) + dot_nt(spread, gate_3)
        gate_rows = jnp.sum(jnp.where(takes, gate_rows, 0.0), axis=1, keepdims=True)
        takes = jnp.where(takes, 1.0, 0.0).astype(BF)
        send_g[...] = (dot(takes, grad_ref[...]) * gate_rows).astype(BF)

    def group(e):
        return pl.ds(pl.multiple_of(e * GROUP, GROUP), GROUP)

    def exchange(src, dst, n):
        def one(i, carry):
            peer = (me + i) % ne
            pltpu.make_async_remote_copy(
                src_ref=src.at[group(peer)],
                dst_ref=dst.at[group(me)],
                send_sem=a2a_send.at[n],
                recv_sem=a2a_recv.at[n],
                device_id=(peer, tt),
                device_id_type=MESH,
            ).start()
            return carry

        lax.fori_loop(1, ne, one, 0)
        dst[group(me), :] = src[group(me), :]

    def exchanged(src, dst, n):
        all_but_one = pl.ds(0, span - GROUP)
        return remote(src.at[all_but_one], dst.at[all_but_one], a2a_send.at[n], a2a_recv.at[n], other)

    exchange(send_g, recv_g, 0)

    packed, padded = GROUP * cap, GROUP * GROUP

    def selection(row, col):
        return jnp.where((row == cap * (col // GROUP) + col % GROUP) & (col % GROUP < cap), 1.0, 0.0).astype(BF)

    compact = selection(iota((packed, padded), 0), iota((packed, padded), 1))
    expand = selection(iota((padded, packed), 1), iota((padded, packed), 0))

    copy_w.wait()
    copy_ws.wait_recv()

    def forward(d, which, first):
        weights = wext.at[(y + ny - d) % ny]
        chunk = slice(which * quarter, (which + 1) * quarter)
        for part_no, lanes, depth in ((0, slice(0, 256), slice(pad, pad + 256)), (1, slice(wide - 256, wide), slice(0, 256))):
            out = slice(part_no * half + which * quarter, part_no * half + (which + 1) * quarter)
            block = ring[d, chunk, lanes]
            own = dot(block, weights[depth, 0:feat])
            sib = dot(block, weights[depth, feat:])
            acc_own[out, :] = own if first else acc_own[out, :] + own
            acc_sib[out, :] = sib if first else acc_sib[out, :] + sib

    for which in range(2):
        forward(0, which, True)
    for i in range(ny - 3):
        for way in range(2):
            ag[way][i].wait_recv()
            ag[way][i + 2].start()
        for way in range(2):
            _, dst, which = ag_place(way, i)
            forward(dst, which, False)

    exchanged(send_g, recv_g, 0).wait_recv()
    for b in range(ne // GROUP):
        rg[b * packed : (b + 1) * packed, 0:feat] = dot(compact, recv_g[b * padded : (b + 1) * padded, :]).astype(BF)
    copy_rg = remote(rg.at[:, pl.ds(0, feat)], rg.at[:, pl.ds(feat, feat)], sib_send.at[1], sib_recv.at[1], other)
    copy_rg.start()

    for i in range(ny - 3, ny - 1):
        for way in range(2):
            ag[way][i].wait_recv()
            _, dst, which = ag_place(way, i)
            forward(dst, which, False)
    copy_e = remote(acc_sib, sib_in, sib_send.at[2], sib_recv.at[2], other)
    copy_e.start()

    def backward(d):
        weights = wext.at[(y + d) % ny]
        low = dot_nt(rg[0:half, :], weights[pad : pad + 256, :])
        high = dot_nt(rg[half:rows, :], weights[0:256, :])
        part[d, :, 0:128] = low[:, 0:128]
        part[d, :, 128:256] = low[:, 128:256] + high[:, 0:128]
        part[d, :, 256:384] = high[:, 128:256]

    far = ny // 2
    rs, rs_place = [], []
    for way in range(2):
        places = [(far, way)]
        for step in range(1, far):
            d = far - step if way == 0 else far + step
            places += [(d, 1 - way), (d, way)]
        rs_place.append(places + [(0, 1 - way), (0, way)])
        rs.append(
            [
                remote(rs_out.at[way, i], rs_in.at[way, i], rs_send.at[way, i], rs_recv.at[way, i], (right, left)[way])
                for i in range(ny - 1)
            ]
        )

    def rs_step(way, i):
        d, which = rs_place[way][i]
        total = part[d, which * quarter : (which + 1) * quarter, :]
        if i >= 2:
            rs[way][i - 2].wait_recv()
            total = total + rs_in[way, i - 2].astype(F32)
        rs_out[way, i] = total.astype(BF)
        rs[way][i].start()

    copy_rg.wait_recv()
    backward(far)
    rs_step(0, 0)
    rs_step(1, 0)
    backward(far - 1)
    rs_step(0, 1)
    backward(far + 1)
    rs_step(1, 1)

    copy_e.wait_recv()
    for b in range(ne // GROUP):
        block = slice(b * packed, (b + 1) * packed)
        total = (acc_own[block, :] + sib_in[block, :]).astype(BF)
        send_e[b * padded : (b + 1) * padded, :] = dot(expand, total).astype(BF)
    exchange(send_e, recv_e, 1)

    done = {far, far - 1, far + 1}
    for i in range(2, ny - 1):
        for way in range(2):
            d, _ = rs_place[way][i]
            if d not in done:
                backward(d)
                done.add(d)
        for way in range(2):
            rs_step(way, i)
    backward(0)

    with jax.named_scope("combine"):
        spread_t = jnp.where(iota((ne, span), 1) // GROUP == iota((ne, span), 0), 1.0, 0.0).astype(BF)
        place_t = (iota((tok, span), 1) % GROUP).astype(F32)
        takes_t = dot(slot, spread_t) == place_t
        mixing = [jnp.where(takes_t, dot(g, spread_t), 0.0).astype(BF) for g in gate_of]
        exchanged(send_e, recv_e, 1).wait_recv()
        mixed_ref[...] = (
            dot(mixing[0], recv_e[...]) + dot(mixing[1], recv_e[...]) + dot(mixing[2], recv_e[...])
        ).astype(BF)

    rs_own = [None, None]
    for i in range(ny - 3, ny - 1):
        for way in range(2):
            _, which = rs_place[way][i + 2]
            rs[way][i].wait_recv()
            if rs_own[which] is None:
                rs_own[which] = part[0, which * quarter : (which + 1) * quarter, :]
            rs_own[which] = rs_own[which] + rs_in[way, i].astype(F32)
    for which in range(2):
        total = rs_own[which].astype(BF)
        hgrad_ref[which * quarter : (which + 1) * quarter, :] = total[:, 0:cols]
        hgrad_ref[half + which * quarter : half + (which + 1) * quarter, :] = total[:, cols:wide]

    for way in range(2):
        for i in range(ny - 1):
            ag[way][i].wait_send()
            rs[way][i].wait_send()
    for copy in (copy_ws, copy_rg, copy_e):
        copy.wait_send()
    exchanged(send_g, recv_g, 0).wait_send()
    exchanged(send_e, recv_e, 1).wait_send()


def body(routes, gates, hidden, down, out_grad):
    ne, nt = lax.axis_size("expert"), lax.axis_size("tensor")
    ny = nt // 2
    tok, top = routes.shape
    rows, cols = hidden.shape[1:]
    feat = out_grad.shape[1]
    cap = rows // ne
    sizes = (ne, ny, cap, tok, top, rows, cols, feat)
    half, quarter, wide = rows // 2, rows // 4, 2 * cols
    span = ne * GROUP
    vmem, anywhere = pl.BlockSpec(memory_space=pltpu.VMEM), pl.BlockSpec(memory_space=pl.ANY)
    dma = pltpu.SemaphoreType.DMA
    mixed, hgrad = pl.pallas_call(
        functools.partial(kernel, sizes),
        out_shape=(
            jax.ShapeDtypeStruct((tok, feat), BF),
            jax.ShapeDtypeStruct((rows, cols), BF),
        ),
        in_specs=[vmem, vmem, vmem, anywhere, anywhere],
        out_specs=(vmem, vmem),
        scratch_shapes=[
            pltpu.VMEM((rows, cols), BF),
            pltpu.VMEM((ny, 512 - cols, 2 * feat), BF),
            pltpu.VMEM((ny, half, wide), BF),
            pltpu.VMEM((rows, feat), F32),
            pltpu.VMEM((rows, feat), F32),
            pltpu.VMEM((rows, feat), F32),
            pltpu.VMEM((rows, 2 * feat), BF),
            pltpu.VMEM((ny, half, wide), F32),
            pltpu.VMEM((2, ny - 1, quarter, wide), BF),
            pltpu.VMEM((2, ny - 1, quarter, wide), BF),
            pltpu.VMEM((span, feat), BF),
            pltpu.VMEM((span, feat), BF),
            pltpu.VMEM((span, feat), BF),
            pltpu.VMEM((span, feat), BF),
            dma((2,)),
            dma((2, ny - 1)),
            dma((2, ny - 1)),
            dma((2, ny - 1)),
            dma((2, ny - 1)),
            dma((3,)),
            dma((3,)),
            dma((2,)),
            dma((2,)),
        ],
        compiler_params=pltpu.CompilerParams(
            collective_id=0, has_side_effects=True, vmem_limit_bytes=48 * 1024 * 1024
        ),
    )(routes, gates, out_grad, hidden[0], down.reshape(ny, 2, cols, feat))
    return mixed, hgrad[None]


def solution(mesh):
    return jax.shard_map(
        body,
        mesh=mesh,
        in_specs=(
            P("expert", None),
            P("expert", None),
            P("expert", None, "tensor"),
            P("expert", None, "tensor"),
            P("expert", "tensor"),
        ),
        out_specs=(P("expert", "tensor"), P("expert", None, "tensor")),
        check_vma=False,
    )
```

time: 156 us -> 81.3 us (0.52)
  Pallas kernels: 0 us -> 74.1 us
  waiting for transfers between devices: 66.5 us -> 0 us
  blocking collectives: 40.1 us -> 0 us
  starting transfers between devices: 13.9 us -> 0 us
  between operations: 14.1 us -> 0.65 us
  matrix products: 7.97 us -> 0 us
  other arithmetic: 7.17 us -> 0 us
    pallas_call x0 -> x1, Pallas kernels: none -> 74.1 us  [body(): pl.pallas_call(functools.partial(kernel, sizes), out_shape=(jax.ShapeDtyp...]
    all_to_all x1 -> x0, blocking collectives: 40.1 us -> none  [body(): lax.all_to_all(outgoing, 'expert', split_axis=0, concat_axis=0, tiled=True)]
    reduce_scatter x1 -> x0, waiting for transfers between devices: 37.5 us -> none  [body(): lax.psum_scatter(partial_value, 'tensor', scatter_dimension=1, tiled=True)]
    all_to_all x1 -> x0, waiting for transfers between devices: 17.8 us -> none  [body(): lax.all_to_all(expert_out, 'expert', split_axis=0, concat_axis=0, tiled=T...]
    all_to_all x1 -> x0, starting transfers between devices: 13.8 us -> none  [body(): lax.all_to_all(expert_out, 'expert', split_axis=0, concat_axis=0, tiled=T...]
    all_gather x1 -> x0, waiting for transfers between devices: 10.5 us -> none  [body(): lax.all_gather(hidden[0], 'tensor', axis=1, tiled=True)]
    dot_general x2 -> x0, matrix products: 7.97 us -> none  [the longest x1 4.51 us: body(): lax.dot_general(arrived_rows, weights, (((1,), (1,)), ((), ())), preferre...]
    unnamed x4 -> x9, local copies, waits for them, and re-layouts: 1.55 us -> 6.22 us
  transfers between devices with their start and end apart: 3 -> 0, of which waited for: 3 -> 0; matrix products, arithmetic and copies ran while one was open for 12% -> 0% of each run, Pallas kernels for 0% -> 0%
where the time goes in v1:
time: 81.3 us; the launch traced here: 81 us
  Pallas kernels  74.1 us (91%)
  local copies, waits for them, and re-layouts  6.22 us (8%)
    pallas_call x1, Pallas kernels, body(): pl.pallas_call(functools.partial(kernel, sizes), out_shape=(jax.ShapeDtyp...  74.1 us
    unnamed x9, local copies, waits for them, and re-layouts  6.22 us

profile of v1, /device:TPU:1, one launch (start us, length us, event | category | flops | bytes accessed | tf_op | source)
XLA Modules:
  0.0 81.0 jit_solution(13853318762375473560)
XLA Ops:
  0.6 0.8 copy.8.routes_ref
  1.4 0.8 copy.9.gates_ref
  2.2 1.1 %copy.7 = bf16[1,576,192]{2,1,0:T(8,128)(2,1)S(1)} copy(bf16[1,576,192]{1,2,0:T(8,128)(2,1)} %param.7) | data formatting | bytes 442368 | tf_op args[2]
  3.3 0.0 copy-start
  3.3 1.4 %copy-done = bf16[1,3072,256]{2,1,0:T(8,128)(2,1)S(1)} copy-done((bf16[1,3072,256]{2,1,0:T(8,128)(2,1)S(1)}, bf16[1,3072,256]{2,1,0:T(8,128)(2,1)}, u32[]{:S(2)}) %copy-start) | copy-done | bytes 1572888
  4.7 0.0 copy-start.1
  4.7 0.7 copy-done.1
  5.4 74.1 %shard_map.68 = (bf16[48,256]{1,0:T(8,128)(2,1)S(1)}, bf16[576,192]{1,0:T(8,128)(2,1)S(1)}) custom-call(s32[48,8]{1,0:T(8,128)S(1)} %copy.8.routes_ref, f32[48,8]{1,0:T(8,128)S(1)} %copy.9.gates_ref, bf16[48,256]{1,0:T(8,128)(2,1)S(1)} %copy-done.1, bf16[576,192]{1,0:T(8,128)(2,1)S(1)} %bitcast.4, bf16[8,2,192,256]{3,2,1,0:T(8,128)(2,1)S(1)} %bitcast.3), custom_call_target="tpu_custom_call" | custom-call | tf_op jit(solution)/shard_map/pallas_call | solution.py:302
  79.5 0.9 %copy.10 = bf16[1,576,192]{1,2,0:T(8,128)(2,1)} copy(bf16[1,576,192]{2,1,0:T(8,128)(2,1)S(1)} %bitcast.5) | data formatting | bytes 442368
  80.3 0.6 copy.12
Async XLA Ops:
  3.3 1.4 %copy-start = (bf16[1,3072,256]{2,1,0:T(8,128)(2,1)S(1)}, bf16[1,3072,256]{2,1,0:T(8,128)(2,1)}, u32[]{:S(2)}) copy-start(bf16[1,3072,256]{2,1,0:T(8,128)(2,1)} %param.8) | copy-start | bytes 4718596
  4.7 0.7 copy-start.1

commit v2 on v1

v2 whole, which is shorter than its diff:
```python
import functools

import jax
import jax.numpy as jnp
from jax import lax
from jax.experimental import pallas as pl
from jax.experimental.pallas import tpu as pltpu
from jax.sharding import PartitionSpec as P

MESH = pl.DeviceIdType.MESH
GROUP = 16
STRIDE, HALF_STRIDE = 27, 11
BF, F32 = jnp.bfloat16, jnp.float32


def dot(a, b):
    return jnp.dot(a, b, preferred_element_type=F32)


def dot_nt(a, b):
    return lax.dot_general(a, b, (((1,), (1,)), ((), ())), preferred_element_type=F32)


def iota(shape, axis):
    return lax.broadcasted_iota(jnp.int32, shape, axis)


def kernel(
    sizes,
    routes_hbm, gates_hbm, grad_hbm, hidden_hbm, down_hbm,
    mixed_ref, hgrad_ref,
    routes_ref, gates_ref, grad_ref, hin, wext, ring, acc_own, acc_sib, sib_in, rg,
    part, rs_out, rs_in, send_g, recv_g, send_e, recv_e,
    local_sem, ag_send, ag_recv, rs_send, rs_recv, sib_send, sib_recv, a2a_send, a2a_recv,
):
    ne, ny, cap, tok, top, rows, cols, feat = sizes
    half, quarter = rows // 2, rows // 4
    wide = 2 * cols
    pad = 256 - cols
    span = ne * GROUP
    cut = (quarter // 2 + 15) // 16 * 16
    subs = ((0, cut), (cut, quarter - cut))
    me = lax.axis_index("expert")
    tt = lax.axis_index("tensor")
    y, core = tt // 2, tt % 2
    right = ((y + 1) % ny) * 2 + core
    left = ((y + ny - 1) % ny) * 2 + core
    other = y * 2 + (1 - core)

    copy_h = pltpu.make_async_copy(hidden_hbm, hin, local_sem.at[0])
    copy_r = pltpu.make_async_copy(routes_hbm, routes_ref, local_sem.at[1])
    copy_k = pltpu.make_async_copy(gates_hbm, gates_ref, local_sem.at[2])
    copy_o = pltpu.make_async_copy(grad_hbm, grad_ref, local_sem.at[3])
    copy_w = pltpu.make_async_copy(
        down_hbm.at[:, core], wext.at[:, pl.ds(pad, cols), pl.ds(0, feat)], local_sem.at[4]
    )
    for copy in (copy_h, copy_r, copy_k, copy_o, copy_w):
        copy.start()

    barrier = pltpu.get_barrier_semaphore()

    def greet(i, carry):
        pl.semaphore_signal(barrier, inc=1, device_id=((me + i) % ne, tt), device_id_type=MESH)
        return carry

    for peer in (right, left, other):
        pl.semaphore_signal(barrier, inc=1, device_id=(me, peer), device_id_type=MESH)
    lax.fori_loop(1, ne, greet, 0)

    wext[:, 0:pad, :] = jnp.zeros((ny, pad, 2 * feat), BF)
    wext[:, pad + cols :, :] = jnp.zeros((ny, pad, 2 * feat), BF)

    copy_h.wait()
    own_rows = jnp.transpose(hin[...])
    for q in range(4):
        g, side = q // 2, q % 2
        ring[0, g * quarter : (g + 1) * quarter, side * cols : (side + 1) * cols] = own_rows[q * quarter : (q + 1) * quarter, :]

    pl.semaphore_wait(barrier, ne - 1 + 3)

    def remote(src, dst, send, recv, peer):
        return pltpu.make_async_remote_copy(
            src_ref=src, dst_ref=dst, send_sem=send, recv_sem=recv, device_id=(me, peer), device_id_type=MESH
        )

    def ag_place(way, i):
        step, which = i // 2, (i % 2) ^ way
        src, dst = (step, step + 1) if way == 0 else ((ny - step) % ny, ny - 1 - step)
        return src, dst, which

    ag = []
    for way in range(2):
        ag.append([])
        for i in range(ny - 1):
            src, dst, which = ag_place(way, i)
            chunk = pl.ds(which * quarter, quarter)
            ag[way].append(
                remote(ring.at[src, chunk], ring.at[dst, chunk], ag_send.at[way, i], ag_recv.at[way, i], (right, left)[way])
            )
    for i in range(2):
        for way in range(2):
            ag[way][i].start()
    copy_ws = remote(
        down_hbm.at[:, 1 - core],
        wext.at[:, pl.ds(pad, cols), pl.ds(feat, feat)],
        sib_send.at[0],
        sib_recv.at[0],
        other,
    )
    copy_ws.start()

    copy_r.wait()
    copy_k.wait()
    copy_o.wait()
    with jax.named_scope("routing"):
        named = jnp.zeros((ne, tok), F32)
        gate = jnp.zeros((ne, tok), F32)
        for k in range(top):
            hit = routes_ref[k : k + 1, :] == iota((ne, tok), 0)
            named = named + jnp.where(hit, 1.0, 0.0)
            gate = gate + jnp.where(hit, gates_ref[k : k + 1, :], 0.0)
        earlier = jnp.where(iota((tok, tok), 0) < iota((tok, tok), 1), 1.0, 0.0).astype(BF)
        slot = jnp.where(named > 0.5, dot(named.astype(BF), earlier), 100.0)
        gate_1 = gate.astype(BF)
        gate_2 = (gate - gate_1.astype(F32)).astype(BF)
        gate_3 = (gate - gate_1.astype(F32) - gate_2.astype(F32)).astype(BF)

        spread = jnp.where(iota((span, ne), 0) // GROUP == iota((span, ne), 1), 1.0, 0.0).astype(BF)
        place = (iota((span, tok), 0) % GROUP).astype(F32)
        takes = dot(spread, slot.astype(BF)) == place
        gate_rows = dot(spread, gate_1) + dot(spread, gate_2) + dot(spread, gate_3)
        gate_rows = jnp.sum(jnp.where(takes, gate_rows, 0.0), axis=1, keepdims=True)
        takes = jnp.where(takes, 1.0, 0.0).astype(BF)
        send_g[...] = (dot(takes, grad_ref[...]) * gate_rows).astype(BF)

    def group(e):
        return pl.ds(pl.multiple_of(e * GROUP, GROUP), GROUP)

    def exchange(src, dst, n, low, count, stride):
        def one(i, carry):
            peer = low + (me + i * stride) % count

            @pl.when(peer != me)
            def _():
                pltpu.make_async_remote_copy(
                    src_ref=src.at[group(peer)],
                    dst_ref=dst.at[group(me)],
                    send_sem=a2a_send.at[n],
                    recv_sem=a2a_recv.at[n],
                    device_id=(peer, tt),
                    device_id_type=MESH,
                ).start()

            return carry

        lax.fori_loop(0, count, one, 0)

    def exchanged(src, dst, n):
        all_but_one = pl.ds(0, span - GROUP)
        return remote(src.at[all_but_one], dst.at[all_but_one], a2a_send.at[n], a2a_recv.at[n], other)

    exchange(send_g, recv_g, 0, 0, ne, STRIDE)
    recv_g[group(me), :] = send_g[group(me), :]

    packed, padded = GROUP * cap, GROUP * GROUP

    def selection(row, col):
        return jnp.where((row == cap * (col // GROUP) + col % GROUP) & (col % GROUP < cap), 1.0, 0.0).astype(BF)

    compact = selection(iota((packed, padded), 0), iota((packed, padded), 1))
    expand = selection(iota((padded, packed), 1), iota((padded, packed), 0))

    copy_w.wait()
    copy_ws.wait_recv()

    def forward(d, g, first):
        weights = wext.at[(y + ny - d) % ny]
        for side, lanes, depth in ((0, slice(0, 256), slice(pad, pad + 256)), (1, slice(wide - 256, wide), slice(0, 256))):
            out = slice((2 * g + side) * quarter, (2 * g + side + 1) * quarter)
            block = ring[d, g * quarter : (g + 1) * quarter, lanes]
            own = dot(block, weights[depth, 0:feat])
            sib = dot(block, weights[depth, feat:])
            acc_own[out, :] = own if first else acc_own[out, :] + own
            acc_sib[out, :] = sib if first else acc_sib[out, :] + sib

    def ag_hop(i):
        for way in range(2):
            ag[way][i].wait_recv()
            if i + 2 < ny - 1:
                ag[way][i + 2].start()
        for way in range(2):
            _, dst, which = ag_place(way, i)
            forward(dst, which, False)

    copy_e = []
    for g in range(2):
        block = pl.ds(g * half, half)
        copy_e.append(remote(acc_sib.at[block], sib_in.at[block], sib_send.at[2 + g], sib_recv.at[2 + g], other))

    def give_back(g):
        copy_e[g].wait_recv()
        per = ne // GROUP // 2
        for b in range(g * per, (g + 1) * per):
            block = slice(b * packed, (b + 1) * packed)
            total = (acc_own[block, :] + sib_in[block, :]).astype(BF)
            send_e[b * padded : (b + 1) * padded, :] = dot(expand, total).astype(BF)
        exchange(send_e, recv_e, 1, g * (ne // 2), ne // 2, HALF_STRIDE)

        @pl.when(me // (ne // 2) == g)
        def _():
            recv_e[group(me), :] = send_e[group(me), :]

    forward(0, 0, True)
    forward(0, 1, True)
    for i in range(ny - 3):
        ag_hop(i)
    exchanged(send_g, recv_g, 0).wait_recv()
    for b in range(ne // GROUP):
        rg[b * packed : (b + 1) * packed, 0:feat] = dot(compact, recv_g[b * padded : (b + 1) * padded, :]).astype(BF)
    copy_rg = remote(rg.at[:, pl.ds(0, feat)], rg.at[:, pl.ds(feat, feat)], sib_send.at[1], sib_recv.at[1], other)
    copy_rg.start()

    for i in range(ny - 3, ny - 1):
        ag_hop(i)
    for copy in copy_e:
        copy.start()

    def backward(d):
        weights = wext.at[(y + d) % ny]
        for g in range(2):
            out = slice(g * quarter, (g + 1) * quarter)
            low = dot_nt(rg[2 * g * quarter : (2 * g + 1) * quarter, :], weights[pad : pad + 256, :])
            high = dot_nt(rg[(2 * g + 1) * quarter : (2 * g + 2) * quarter, :], weights[0:256, :])
            part[d, out, 0:128] = low[:, 0:128]
            part[d, out, 128:256] = low[:, 128:256] + high[:, 0:128]
            part[d, out, 256:384] = high[:, 128:256]

    far = ny // 2
    rs_place, rs = [], []
    for way in range(2):
        places = [(far, 0, way), (far, 1, way)]
        for step in range(1, far + 1):
            d = (far - step if way == 0 else far + step) % ny
            places += [(d, 0, 1 - way), (d, 1, 1 - way), (d, 0, way), (d, 1, way)]
        rs_place.append(places)
        rs.append({})
        for i, (d, g, which) in enumerate(places):
            if d:
                chunk = pl.ds(0, subs[which][1])
                rs[way][d, g, which] = (
                    i,
                    remote(
                        rs_out.at[way, i, chunk], rs_in.at[way, i, chunk],
                        rs_send.at[way, i], rs_recv.at[way, i], (right, left)[way],
                    ),
                )

    def rs_share(d, g, which):
        first, size = subs[which]
        return part[d, g * quarter + first : g * quarter + first + size, :]

    def rs_arrived(way, d, g, which):
        before = ((d + 1) if way == 0 else (d + ny - 1) % ny, g, which)
        if before not in rs[way]:
            return None
        i, copy = rs[way][before]
        copy.wait_recv()
        return rs_in[way, i, 0 : subs[which][1], :].astype(F32)

    def rs_step(way, n):
        d, g, which = rs_place[way][n]
        arrived = rs_arrived(way, d, g, which)
        total = rs_share(d, g, which)
        if arrived is not None:
            total = total + arrived
        i, copy = rs[way][d, g, which]
        rs_out[way, i, 0 : subs[which][1], :] = total.astype(BF)
        copy.start()

    copy_rg.wait_recv()
    backward(far)
    for n in range(2):
        for way in range(2):
            rs_step(way, n)
    backward(far - 1)
    for n in range(2, 4):
        rs_step(0, n)
    backward(far + 1)
    for n in range(2, 4):
        rs_step(1, n)
    give_back(0)
    give_back(1)
    backward(far - 2)
    backward(far + 2)

    done = {far, far - 1, far + 1, far - 2, far + 2}
    def rs_both(n):
        for way in range(2):
            d = rs_place[way][n][0]
            if d not in done:
                backward(d)
                done.add(d)
            rs_step(way, n)

    for n in range(4, 4 * far - 2):
        rs_both(n)
    backward(0)

    with jax.named_scope("combine"):
        slot_t = jnp.transpose(slot).astype(BF)
        gate_t = jnp.transpose(gate)
        gate_1 = gate_t.astype(BF)
        gate_2 = (gate_t - gate_1.astype(F32)).astype(BF)
        gate_3 = (gate_t - gate_1.astype(F32) - gate_2.astype(F32)).astype(BF)
        spread_t = jnp.where(iota((ne, span), 1) // GROUP == iota((ne, span), 0), 1.0, 0.0).astype(BF)
        place_t = (iota((tok, span), 1) % GROUP).astype(F32)
        takes_t = dot(slot_t, spread_t) == place_t
        mixing = [jnp.where(takes_t, dot(g, spread_t), 0.0).astype(BF) for g in (gate_1, gate_2, gate_3)]
        exchanged(send_e, recv_e, 1).wait_recv()
        mixed_ref[...] = (
            dot(mixing[0], recv_e[...]) + dot(mixing[1], recv_e[...]) + dot(mixing[2], recv_e[...])
        ).astype(BF)

    last = {}
    for n in range(4 * far - 2, 4 * far + 2):
        for way in range(2):
            _, g, which = rs_place[way][n]
            if (g, which) not in last:
                last[g, which] = rs_share(0, g, which)
            last[g, which] = last[g, which] + rs_arrived(way, 0, g, which)
    for (g, which), total in last.items():
        first, size = subs[which]
        total = total.astype(BF)
        for side in range(2):
            at = (2 * g + side) * quarter + first
            hgrad_ref[at : at + size, :] = total[:, side * cols : (side + 1) * cols]

    for way in range(2):
        for copy in ag[way]:
            copy.wait_send()
        for _, copy in rs[way].values():
            copy.wait_send()
    for copy in (copy_ws, copy_rg, copy_e[0], copy_e[1]):
        copy.wait_send()
    exchanged(send_g, recv_g, 0).wait_send()
    exchanged(send_e, recv_e, 1).wait_send()


def body(routes, gates, hidden, down, out_grad):
    ne, nt = lax.axis_size("expert"), lax.axis_size("tensor")
    ny = nt // 2
    tok, top = routes.shape
    rows, cols = hidden.shape[1:]
    feat = out_grad.shape[1]
    cap = rows // ne
    sizes = (ne, ny, cap, tok, top, rows, cols, feat)
    half, wide = rows // 2, 2 * cols
    sub = (rows // 8 + 15) // 16 * 16
    span = ne * GROUP
    vmem, hbm = pl.BlockSpec(memory_space=pltpu.VMEM), pl.BlockSpec(memory_space=pltpu.HBM)
    dma = pltpu.SemaphoreType.DMA
    mixed, hgrad = pl.pallas_call(
        functools.partial(kernel, sizes),
        out_shape=(
            jax.ShapeDtypeStruct((tok, feat), BF),
            jax.ShapeDtypeStruct((rows, cols), BF),
        ),
        in_specs=[hbm] * 5,
        out_specs=(vmem, vmem),
        scratch_shapes=[
            pltpu.VMEM((top, tok), jnp.int32),
            pltpu.VMEM((top, tok), F32),
            pltpu.VMEM((tok, feat), BF),
            pltpu.VMEM((cols, rows), BF),
            pltpu.VMEM((ny, 512 - cols, 2 * feat), BF),
            pltpu.VMEM((ny, half, wide), BF),
            pltpu.VMEM((rows, feat), F32),
            pltpu.VMEM((rows, feat), F32),
            pltpu.VMEM((rows, feat), F32),
            pltpu.VMEM((rows, 2 * feat), BF),
            pltpu.VMEM((ny, half, wide), F32),
            pltpu.VMEM((2, 2 * ny - 2, sub, wide), BF),
            pltpu.VMEM((2, 2 * ny - 2, sub, wide), BF),
            pltpu.VMEM((span, feat), BF),
            pltpu.VMEM((span, feat), BF),
            pltpu.VMEM((span, feat), BF),
            pltpu.VMEM((span, feat), BF),
            dma((5,)),
            dma((2, ny - 1)),
            dma((2, ny - 1)),
            dma((2, 2 * ny - 2)),
            dma((2, 2 * ny - 2)),
            dma((4,)),
            dma((4,)),
            dma((2,)),
            dma((2,)),
        ],
        compiler_params=pltpu.CompilerParams(
            collective_id=0, has_side_effects=True, vmem_limit_bytes=48 * 1024 * 1024
        ),
    )(*[pltpu.with_memory_space_constraint(a, pltpu.HBM) for a in (routes.T, gates.T, out_grad, hidden[0].T, down.reshape(ny, 2, cols, feat))])
    return mixed, hgrad[None]


def solution(mesh):
    return jax.shard_map(
        body,
        mesh=mesh,
        in_specs=(
            P("expert", None),
            P("expert", None),
            P("expert", None, "tensor"),
            P("expert", None, "tensor"),
            P("expert", "tensor"),
        ),
        out_specs=(P("expert", "tensor"), P("expert", None, "tensor")),
        check_vma=False,
    )
```

time: 81.3 us -> 66.4 us (0.82)
  Pallas kernels: 74.1 us -> 64.2 us
  local copies, waits for them, and re-layouts: 6.22 us -> 1.46 us
    pallas_call x1, Pallas kernels: 74.1 us -> 64.2 us  [body(): pl.pallas_call(functools.partial(kernel, sizes), out_shape=(jax.ShapeDtyp...]
    unnamed x9 -> x2, local copies, waits for them, and re-layouts: 6.22 us -> 1.46 us
where the time goes in v2:
time: 66.4 us; the launch traced here: 66.3 us
  Pallas kernels  64.2 us (97%)
  local copies, waits for them, and re-layouts  1.46 us (2%)
    pallas_call x1, Pallas kernels, body(): pl.pallas_call(functools.partial(kernel, sizes), out_shape=(jax.ShapeDtyp...  64.2 us
    unnamed x2, local copies, waits for them, and re-layouts  1.46 us

profile of v2, /device:TPU:1, one launch (start us, length us, event | category | flops | bytes accessed | tf_op | source)
XLA Modules:
  0.0 66.3 jit_solution(5298028356237129927)
XLA Ops:
  0.6 64.2 %shard_map.68 = (bf16[48,256]{1,0:T(8,128)(2,1)S(1)}, bf16[576,192]{1,0:T(8,128)(2,1)S(1)}) custom-call(s32[8,48]{1,0:T(8,128)} %bitcast.10, f32[8,48]{1,0:T(8,128)} %bitcast.11, bf16[48,256]{1,0:T(8,128)(2,1)} %grad_hbm.1, bf16[192,576]{1,0:T(8,128)(2,1)} %bitcast.9, bf16[8,2,192,256]{3,2,1,0:T(8,128)(2,1)} %bitcast.8), custom_call_target="tpu_custom_call" | custom-call | tf_op jit(solution)/shard_map/pallas_call | solution.py:362
  64.8 0.9 %copy.7 = bf16[1,576,192]{1,2,0:T(8,128)(2,1)} copy(bf16[1,576,192]{2,1,0:T(8,128)(2,1)S(1)} %bitcast.7) | data formatting | bytes 442368
  65.7 0.6 copy.9

commit v3 on v2

v3 whole, which is shorter than its diff:
```python
import functools

import jax
import jax.numpy as jnp
from jax import lax
from jax.experimental import pallas as pl
from jax.experimental.pallas import tpu as pltpu
from jax.sharding import PartitionSpec as P

MESH = pl.DeviceIdType.MESH
GROUP = 48
STRIDE = 11
BF, F32 = jnp.bfloat16, jnp.float32


def dot(a, b):
    return jnp.dot(a, b, preferred_element_type=F32)


def dot_nt(a, b):
    return lax.dot_general(a, b, (((1,), (1,)), ((), ())), preferred_element_type=F32)


def iota(shape, axis):
    return lax.broadcasted_iota(jnp.int32, shape, axis)


def lane_groups(count, width):
    lane = iota((1, count * width), 1)
    group = jnp.zeros((1, count * width), jnp.int32)
    for m in range(1, count):
        group = group + jnp.where(lane >= m * width, 1, 0)
    return group, lane - group * width


def kernel(
    sizes,
    routes_hbm, gates_hbm, grad_hbm, hidden_hbm, down_hbm,
    mixed_ref, hgrad_ref,
    routes_ref, gates_ref, grads, hin, wext, ring, acc, sib_in, rg,
    part, rs_out, rs_in, send_g, recv_g, send_e, recv_e, mix_part, mix_in,
    local_sem, ag_send, ag_recv, rs_send, rs_recv, sib_send, sib_recv, a2a_send, a2a_recv,
):
    ne, ny, cap, tok, top, rows, cols, feat = sizes
    half, quarter = rows // 2, rows // 4
    wide = 2 * cols
    pad = 256 - cols
    peers = ne // 2
    span = peers * GROUP
    tiles = 2 * feat // 128
    cut = (quarter // 2 + 15) // 16 * 16
    subs = ((0, cut), (cut, quarter - cut))
    me = lax.axis_index("expert")
    tt = lax.axis_index("tensor")
    y, core = tt // 2, tt % 2
    right = ((y + 1) % ny) * 2 + core
    left = ((y + ny - 1) % ny) * 2 + core
    other = y * 2 + (1 - core)
    reach = (me // peers + core) % 2
    rows_at = pl.multiple_of(reach * half, 16)
    rows_other = pl.multiple_of((1 - reach) * half, 16)
    own_feat = pl.multiple_of(core * feat, 128)

    copy_h = pltpu.make_async_copy(hidden_hbm, hin, local_sem.at[0])
    copy_r = pltpu.make_async_copy(routes_hbm, routes_ref, local_sem.at[1])
    copy_k = pltpu.make_async_copy(gates_hbm, gates_ref, local_sem.at[2])
    copy_w = pltpu.make_async_copy(
        down_hbm.at[:, core], wext.at[:, pl.ds(pad, cols), pl.ds(own_feat, feat)], local_sem.at[3]
    )
    grad_tiles = []
    for i in range(feat // 128):
        at = pl.multiple_of((core * (feat // 128) + i) * tok, 16)
        grad_tiles.append((grad_hbm.at[:, pl.ds(i * 128, 128)], grads.at[pl.ds(at, tok)]))
    copy_o = [pltpu.make_async_copy(src, dst, local_sem.at[4 + i]) for i, (src, dst) in enumerate(grad_tiles)]
    for copy in (copy_h, copy_r, copy_k, *copy_o, copy_w):
        copy.start()

    barrier = pltpu.get_barrier_semaphore()

    def greet(i, carry):
        peer = reach * peers + (me + i) % peers

        @pl.when(peer != me)
        def _():
            pl.semaphore_signal(barrier, inc=1, device_id=(peer, tt), device_id_type=MESH)

        return carry

    for peer in (right, left, other):
        pl.semaphore_signal(barrier, inc=1, device_id=(me, peer), device_id_type=MESH)
    lax.fori_loop(0, peers, greet, 0, unroll=8)

    wext[:, 0:pad, :] = jnp.zeros((ny, pad, 2 * feat), BF)
    wext[:, pad + cols :, :] = jnp.zeros((ny, pad, 2 * feat), BF)

    copy_h.wait()
    own_rows = jnp.transpose(hin[...])
    for q in range(4):
        g, side = q // 2, q % 2
        ring[0, g * quarter : (g + 1) * quarter, side * cols : (side + 1) * cols] = own_rows[q * quarter : (q + 1) * quarter, :]

    pl.semaphore_wait(barrier, peers - 1 + core + 3)

    def remote(src, dst, send, recv, peer):
        return pltpu.make_async_remote_copy(
            src_ref=src, dst_ref=dst, send_sem=send, recv_sem=recv, device_id=(me, peer), device_id_type=MESH
        )

    def ag_place(way, i):
        step, which = i // 2, (i % 2) ^ way
        src, dst = (step, step + 1) if way == 0 else ((ny - step) % ny, ny - 1 - step)
        return src, dst, which

    ag = []
    for way in range(2):
        ag.append([])
        for i in range(ny - 1):
            src, dst, which = ag_place(way, i)
            chunk = pl.ds(which * quarter, quarter)
            ag[way].append(
                remote(ring.at[src, chunk], ring.at[dst, chunk], ag_send.at[way, i], ag_recv.at[way, i], (right, left)[way])
            )
    for i in range(2):
        for way in range(2):
            ag[way][i].start()
    copy_os = [remote(src, dst, sib_send.at[3 + i], sib_recv.at[3 + i], other) for i, (src, dst) in enumerate(grad_tiles)]
    for copy in copy_os:
        copy.start()
    copy_ws = remote(
        down_hbm.at[:, 1 - core],
        wext.at[:, pl.ds(pad, cols), pl.ds(own_feat, feat)],
        sib_send.at[0],
        sib_recv.at[0],
        other,
    )
    copy_ws.start()

    copy_r.wait()
    copy_k.wait()
    with jax.named_scope("routing"):
        named = jnp.zeros((ne, tok), F32)
        gate = jnp.zeros((ne, tok), F32)
        for k in range(top):
            hit = routes_ref[k : k + 1, :] == iota((ne, tok), 0)
            named = named + jnp.where(hit, 1.0, 0.0)
            gate = gate + jnp.where(hit, gates_ref[k : k + 1, :], 0.0)
        earlier = jnp.where(iota((tok, tok), 0) < iota((tok, tok), 1), 1.0, 0.0).astype(BF)
        slot = jnp.where(named > 0.5, dot(named.astype(BF), earlier), 100.0)
        token, lane = iota((tok, tiles * tok), 0), iota((tok, tiles * tok), 1)
        repeat = jnp.zeros((tok, tiles * tok), F32)
        offset = jnp.zeros((1, tiles * tok), F32)
        for j in range(tiles):
            repeat = repeat + jnp.where(lane == token + j * tok, 1.0, 0.0)
            offset = offset + jnp.where(lane[0:1, :] >= (j + 1) * tok, float(cap), 0.0)
        repeat = repeat.astype(BF)

        def thirds(x):
            first = x.astype(BF)
            second = (x - first.astype(F32)).astype(BF)
            return first, second, (x - first.astype(F32) - second.astype(F32)).astype(BF)

        slot_4 = dot(slot.astype(BF), repeat) + offset
        gate_4 = sum(dot(g, repeat) for g in thirds(gate))
        spread = iota((peers, GROUP, ne), 2) == iota((peers, GROUP, ne), 0) + reach * peers
        spread = jnp.where(spread, 1.0, 0.0).reshape(span, ne).astype(BF)
        place = iota((peers, GROUP, tiles * tok), 1).reshape(span, tiles * tok).astype(F32)
        takes = dot(spread, slot_4.astype(BF)) == place
        gate_rows = sum(dot(spread, g) for g in thirds(gate_4))
        gate_rows = jnp.sum(jnp.where(takes, gate_rows, 0.0), axis=1, keepdims=True)
        takes = jnp.where(takes, 1.0, 0.0).astype(BF)
        for copy in copy_o:
            copy.wait()
        for copy in copy_os:
            copy.wait_recv()
        send_g[...] = (dot(takes, grads[...]) * gate_rows).astype(BF)

    def group(u):
        return pl.ds(pl.multiple_of(u * GROUP, 16), GROUP)

    own_group = group(me % peers)

    def exchange(src, dst, n):
        def one(i, carry):
            u = (me + i * STRIDE) % peers
            peer = reach * peers + u

            @pl.when(peer != me)
            def _():
                pltpu.make_async_remote_copy(
                    src_ref=src.at[group(u)],
                    dst_ref=dst.at[own_group],
                    send_sem=a2a_send.at[n],
                    recv_sem=a2a_recv.at[n],
                    device_id=(peer, tt),
                    device_id_type=MESH,
                ).start()

            return carry

        lax.fori_loop(0, peers, one, 0)

        @pl.when(core == 0)
        def _():
            dst[own_group, :] = src[own_group, :]

    def exchanged(src, dst, n, wait):
        for c in range(2):

            @pl.when(core == c)
            def _(c=c):
                every = pl.ds(0, span - (1 - c) * GROUP)
                getattr(remote(src.at[every], dst.at[every], a2a_send.at[n], a2a_recv.at[n], other), wait)()

    exchange(send_g, recv_g, 0)

    packed, padded = 16 * cap, 16 * GROUP
    pair, row = lane_groups(16, GROUP)
    compact, expand = [], []
    for j in range(tiles):
        at = row - j * cap
        named_row = jnp.where((at >= 0) & (at < cap), pair * cap + at, -1)
        compact.append(jnp.where(iota((packed, padded), 0) == named_row, 1.0, 0.0).astype(BF))
        at = iota((16, GROUP, packed), 1) - j * cap
        hit = (iota((16, GROUP, packed), 2) == iota((16, GROUP, packed), 0) * cap + at) & (at >= 0) & (at < cap)
        expand.append(jnp.where(hit, 1.0, 0.0).reshape(padded, packed).astype(BF))

    copy_w.wait()
    copy_ws.wait_recv()

    def forward(d, g, first):
        weights = wext.at[(y + ny - d) % ny]
        for side, lanes, depth in ((0, slice(0, 256), slice(pad, pad + 256)), (1, slice(wide - 256, wide), slice(0, 256))):
            out = slice((2 * g + side) * quarter, (2 * g + side + 1) * quarter)
            block = ring[d, g * quarter : (g + 1) * quarter, lanes]
            share = dot(block, weights[depth, :])
            acc[out, :] = share if first else acc[out, :] + share

    def ag_hop(i):
        for way in range(2):
            ag[way][i].wait_recv()
            if i + 2 < ny - 1:
                ag[way][i + 2].start()
        for way in range(2):
            _, dst, which = ag_place(way, i)
            forward(dst, which, False)

    copy_e = remote(acc.at[pl.ds(rows_other, half)], sib_in, sib_send.at[2], sib_recv.at[2], other)

    def give_back():
        copy_e.wait_recv()
        for b in range(peers // 16):
            total = (acc[pl.ds(rows_at + b * packed, packed), :] + sib_in[b * packed : (b + 1) * packed, :]).astype(BF)
            out = sum(dot(expand[j], total[:, j * 128 : (j + 1) * 128]) for j in range(tiles))
            send_e[b * padded : (b + 1) * padded, :] = out.astype(BF)
        exchange(send_e, recv_e, 1)

    forward(0, 0, True)
    forward(0, 1, True)
    for i in range(ny - 5):
        ag_hop(i)
    ag_hop(3)
    ag_hop(4)
    exchanged(send_g, recv_g, 0, "wait_recv")
    for b in range(peers // 16):
        arrived = recv_g[b * padded : (b + 1) * padded, :]
        for j in range(tiles):
            rg[pl.ds(rows_at + b * packed, packed), j * 128 : (j + 1) * 128] = dot(compact[j], arrived).astype(BF)
    rg_half = rg.at[pl.ds(rows_at, half)]
    copy_rg = remote(rg_half, rg_half, sib_send.at[1], sib_recv.at[1], other)
    copy_rg.start()

    ag_hop(5)
    def backward(d):
        weights = wext.at[(y + d) % ny]
        for g in range(2):
            out = slice(g * quarter, (g + 1) * quarter)
            low = dot_nt(rg[2 * g * quarter : (2 * g + 1) * quarter, :], weights[pad : pad + 256, :])
            high = dot_nt(rg[(2 * g + 1) * quarter : (2 * g + 2) * quarter, :], weights[0:256, :])
            part[d, out, 0:128] = low[:, 0:128]
            part[d, out, 128:256] = low[:, 128:256] + high[:, 0:128]
            part[d, out, 256:384] = high[:, 128:256]

    far = ny // 2
    rs_place, rs = [], []
    for way in range(2):
        places = [(far, 0, way), (far, 1, way)]
        for step in range(1, far + 1):
            d = (far - step if way == 0 else far + step) % ny
            places += [(d, 0, 1 - way), (d, 1, 1 - way), (d, 0, way), (d, 1, way)]
        rs_place.append(places)
        rs.append({})
        for i, (d, g, which) in enumerate(places):
            if d:
                chunk = pl.ds(0, subs[which][1])
                rs[way][d, g, which] = (
                    i,
                    remote(
                        rs_out.at[way, i, chunk], rs_in.at[way, i, chunk],
                        rs_send.at[way, i], rs_recv.at[way, i], (right, left)[way],
                    ),
                )

    def rs_share(d, g, which):
        first, size = subs[which]
        return part[d, g * quarter + first : g * quarter + first + size, :]

    def rs_arrived(way, d, g, which):
        before = ((d + 1) if way == 0 else (d + ny - 1) % ny, g, which)
        if before not in rs[way]:
            return None
        i, copy = rs[way][before]
        copy.wait_recv()
        return rs_in[way, i, 0 : subs[which][1], :].astype(F32)

    def rs_step(way, n):
        d, g, which = rs_place[way][n]
        arrived = rs_arrived(way, d, g, which)
        total = rs_share(d, g, which)
        if arrived is not None:
            total = total + arrived
        i, copy = rs[way][d, g, which]
        rs_out[way, i, 0 : subs[which][1], :] = total.astype(BF)
        copy.start()

    copy_rg.wait_recv()
    backward(far)
    for n in range(2):
        for way in range(2):
            rs_step(way, n)
    backward(far - 1)
    for n in range(2, 4):
        rs_step(0, n)
    backward(far + 1)
    for n in range(2, 4):
        rs_step(1, n)
    ag_hop(6)
    copy_e.start()
    backward(far - 2)
    backward(far + 2)
    give_back()

    done = {far, far - 1, far + 1, far - 2, far + 2}
    def rs_both(n):
        for way in range(2):
            d = rs_place[way][n][0]
            if d not in done:
                backward(d)
                done.add(d)
            rs_step(way, n)

    for n in range(4, 4 * far - 2):
        rs_both(n)
    backward(0)

    with jax.named_scope("combine"):
        pair, row = lane_groups(peers, GROUP)
        spread_t = jnp.where(iota((ne, span), 0) == pair + reach * peers, 1.0, 0.0).astype(BF)
        takes_t = dot(jnp.transpose(slot_4).astype(BF), spread_t) == row.astype(F32)
        mixing = [jnp.where(takes_t, dot(g, spread_t), 0.0).astype(BF) for g in thirds(jnp.transpose(gate_4))]
    exchanged(send_e, recv_e, 1, "wait_recv")
    arrived = recv_e[...]
    mix_part[...] = dot(mixing[0], arrived) + dot(mixing[1], arrived) + dot(mixing[2], arrived)
    mix_rows = tiles // 2 * tok
    copy_m = remote(
        mix_part.at[pl.ds(pl.multiple_of((1 - core) * mix_rows, 16), mix_rows)], mix_in, sib_send.at[5], sib_recv.at[5], other
    )
    copy_m.start()

    last = {}
    for n in range(4 * far - 2, 4 * far + 2):
        for way in range(2):
            _, g, which = rs_place[way][n]
            if (g, which) not in last:
                last[g, which] = rs_share(0, g, which)
            last[g, which] = last[g, which] + rs_arrived(way, 0, g, which)
    for (g, which), total in last.items():
        first, size = subs[which]
        total = total.astype(BF)
        for side in range(2):
            at = (2 * g + side) * quarter + first
            hgrad_ref[at : at + size, :] = total[:, side * cols : (side + 1) * cols]

    copy_m.wait_recv()
    mixed = (mix_part[pl.ds(pl.multiple_of(core * mix_rows, 16), mix_rows), :] + mix_in[...]).astype(BF)
    for i in range(tiles // 2):
        mixed_ref[:, i * 128 : (i + 1) * 128] = mixed[i * tok : (i + 1) * tok, :]

    for way in range(2):
        for copy in ag[way]:
            copy.wait_send()
        for _, copy in rs[way].values():
            copy.wait_send()
    for copy in (copy_ws, copy_rg, copy_e, copy_m, *copy_os):
        copy.wait_send()
    exchanged(send_g, recv_g, 0, "wait_send")
    exchanged(send_e, recv_e, 1, "wait_send")


def body(routes, gates, hidden, down, out_grad):
    ne, nt = lax.axis_size("expert"), lax.axis_size("tensor")
    ny = nt // 2
    tok, top = routes.shape
    rows, cols = hidden.shape[1:]
    feat = out_grad.shape[1]
    cap = rows // ne
    sizes = (ne, ny, cap, tok, top, rows, cols, feat)
    half, wide = rows // 2, 2 * cols
    sub = (rows // 8 + 15) // 16 * 16
    span = ne // 2 * GROUP
    vmem, hbm = pl.BlockSpec(memory_space=pltpu.VMEM), pl.BlockSpec(memory_space=pltpu.HBM)
    dma = pltpu.SemaphoreType.DMA
    mixed, hgrad = pl.pallas_call(
        functools.partial(kernel, sizes),
        out_shape=(
            jax.ShapeDtypeStruct((tok, feat), BF),
            jax.ShapeDtypeStruct((rows, cols), BF),
        ),
        in_specs=[hbm] * 5,
        out_specs=(vmem, vmem),
        scratch_shapes=[
            pltpu.VMEM((top, tok), jnp.int32),
            pltpu.VMEM((top, tok), F32),
            pltpu.VMEM((feat // 64 * tok, 128), BF),
            pltpu.VMEM((cols, rows), BF),
            pltpu.VMEM((ny, 512 - cols, 2 * feat), BF),
            pltpu.VMEM((ny, half, wide), BF),
            pltpu.VMEM((rows, 2 * feat), F32),
            pltpu.VMEM((half, 2 * feat), F32),
            pltpu.VMEM((rows, 2 * feat), BF),
            pltpu.VMEM((ny, half, wide), F32),
            pltpu.VMEM((2, 2 * ny - 2, sub, wide), BF),
            pltpu.VMEM((2, 2 * ny - 2, sub, wide), BF),
            pltpu.VMEM((span, 128), BF),
            pltpu.VMEM((span, 128), BF),
            pltpu.VMEM((span, 128), BF),
            pltpu.VMEM((span, 128), BF),
            pltpu.VMEM((feat // 64 * tok, 128), F32),
            pltpu.VMEM((feat // 128 * tok, 128), F32),
            dma((4 + feat // 128,)),
            dma((2, ny - 1)),
            dma((2, ny - 1)),
            dma((2, 2 * ny - 2)),
            dma((2, 2 * ny - 2)),
            dma((6,)),
            dma((6,)),
            dma((2,)),
            dma((2,)),
        ],
        compiler_params=pltpu.CompilerParams(
            collective_id=0, has_side_effects=True, vmem_limit_bytes=48 * 1024 * 1024
        ),
    )(*[pltpu.with_memory_space_constraint(a, pltpu.HBM) for a in (routes.T, gates.T, out_grad, hidden[0].T, down.reshape(ny, 2, cols, feat))])
    return mixed, hgrad[None]


def solution(mesh):
    return jax.shard_map(
        body,
        mesh=mesh,
        in_specs=(
            P("expert", None),
            P("expert", None),
            P("expert", None, "tensor"),
            P("expert", None, "tensor"),
            P("expert", "tensor"),
        ),
        out_specs=(P("expert", "tensor"), P("expert", None, "tensor")),
        check_vma=False,
    )
```

time: 66.4 us -> 64.2 us (0.967)
  Pallas kernels: 64.2 us -> 62 us
    pallas_call x1, Pallas kernels: 64.2 us -> 62 us  [body(): pl.pallas_call(functools.partial(kernel, sizes), out_shape=(jax.ShapeDtyp...]
where the time goes in v3:
time: 64.2 us; the launch traced here: 64.1 us
  Pallas kernels  62 us (97%)
  local copies, waits for them, and re-layouts  1.46 us (2%)
    pallas_call x1, Pallas kernels, body(): pl.pallas_call(functools.partial(kernel, sizes), out_shape=(jax.ShapeDtyp...  62 us
    unnamed x2, local copies, waits for them, and re-layouts  1.46 us

profile of v3, /device:TPU:1, one launch (start us, length us, event | category | flops | bytes accessed | tf_op | source)
XLA Modules:
  0.0 64.1 jit_solution(4742115282365842573)
XLA Ops:
  0.6 62.0 %shard_map.68 = (bf16[48,256]{1,0:T(8,128)(2,1)S(1)}, bf16[576,192]{1,0:T(8,128)(2,1)S(1)}) custom-call(s32[8,48]{1,0:T(8,128)} %bitcast.10, f32[8,48]{1,0:T(8,128)} %bitcast.11, bf16[48,256]{1,0:T(8,128)(2,1)} %grad_hbm.1, bf16[192,576]{1,0:T(8,128)(2,1)} %bitcast.9, bf16[8,2,192,256]{3,2,1,0:T(8,128)(2,1)} %bitcast.8), custom_call_target="tpu_custom_call" | custom-call | tf_op jit(solution)/shard_map/pallas_call | solution.py:412
  62.6 0.9 %copy.7 = bf16[1,576,192]{1,2,0:T(8,128)(2,1)} copy(bf16[1,576,192]{2,1,0:T(8,128)(2,1)S(1)} %bitcast.7) | data formatting | bytes 442368
  63.4 0.6 copy.9

commit v4 on v3

--- a/solution.py
+++ b/solution.py
@@ -39,7 +39,7 @@
     mixed_ref, hgrad_ref,
     routes_ref, gates_ref, grads, hin, wext, ring, acc, sib_in, rg,
     part, rs_out, rs_in, send_g, recv_g, send_e, recv_e, mix_part, mix_in,
-    local_sem, ag_send, ag_recv, rs_send, rs_recv, sib_send, sib_recv, a2a_send, a2a_recv,
+    ready_sem, local_sem, ag_send, ag_recv, rs_send, rs_recv, sib_send, sib_recv, a2a_send, a2a_recv,
 ):
     ne, ny, cap, tok, top, rows, cols, feat = sizes
     half, quarter = rows // 2, rows // 4
@@ -86,8 +86,13 @@
 
         return carry
 
-    for peer in (right, left, other):
-        pl.semaphore_signal(barrier, inc=1, device_id=(me, peer), device_id_type=MESH)
+    for chip in (right, left):
+        pl.semaphore_signal(barrier, inc=1, device_id=(me, chip // 2 * 2), device_id_type=MESH)
+
+    @pl.when(core == 1)
+    def _():
+        pl.semaphore_signal(barrier, inc=1, device_id=(me, other), device_id_type=MESH)
+
     lax.fori_loop(0, peers, greet, 0, unroll=8)
 
     wext[:, 0:pad, :] = jnp.zeros((ny, pad, 2 * feat), BF)
@@ -99,7 +104,15 @@
         g, side = q // 2, q % 2
         ring[0, g * quarter : (g + 1) * quarter, side * cols : (side + 1) * cols] = own_rows[q * quarter : (q + 1) * quarter, :]
 
-    pl.semaphore_wait(barrier, peers - 1 + core + 3)
+    @pl.when(core == 0)
+    def _():
+        pl.semaphore_wait(barrier, peers - 1 + 5)
+        pl.semaphore_signal(ready_sem, inc=1, device_id=(me, other), device_id_type=MESH)
+
+    @pl.when(core == 1)
+    def _():
+        pl.semaphore_wait(ready_sem, 1)
+
 
     def remote(src, dst, send, recv, peer):
         return pltpu.make_async_remote_copy(
@@ -211,7 +224,20 @@
                 every = pl.ds(0, span - (1 - c) * GROUP)
                 getattr(remote(src.at[every], dst.at[every], a2a_send.at[n], a2a_recv.at[n], other), wait)()
 
-    exchange(send_g, recv_g, 0)
+    early = me < peers
+
+    def exchange_far():
+        pl.semaphore_wait(barrier, peers)
+        exchange(send_g, recv_g, 0)
+
+    @pl.when(core == 0)
+    def _():
+        exchange(send_g, recv_g, 0)
+
+    @pl.when((core == 1) & jnp.logical_not(early))
+    def _():
+        exchange_far()
+
 
     packed, padded = 16 * cap, 16 * GROUP
     pair, row = lane_groups(16, GROUP)
@@ -256,10 +282,14 @@
 
     forward(0, 0, True)
     forward(0, 1, True)
-    for i in range(ny - 5):
+    for i in range(ny - 3):
         ag_hop(i)
-    ag_hop(3)
-    ag_hop(4)
+        if i == 0:
+
+            @pl.when((core == 1) & early)
+            def _():
+                exchange_far()
+
     exchanged(send_g, recv_g, 0, "wait_recv")
     for b in range(peers // 16):
         arrived = recv_g[b * padded : (b + 1) * padded, :]
@@ -436,6 +466,7 @@
             pltpu.VMEM((span, 128), BF),
             pltpu.VMEM((feat // 64 * tok, 128), F32),
             pltpu.VMEM((feat // 128 * tok, 128), F32),
+            pltpu.SemaphoreType.REGULAR,
             dma((4 + feat // 128,)),
             dma((2, ny - 1)),
             dma((2, ny - 1)),

time: 64.2 us -> 64.8 us (level)
  no operation moved by 1% of the time
where the time goes in v4:
time: 64.8 us; the launch traced here: 64.6 us
  Pallas kernels  62.5 us (96%)
  local copies, waits for them, and re-layouts  1.46 us (2%)
    pallas_call x1, Pallas kernels, body(): pl.pallas_call(functools.partial(kernel, sizes), out_shape=(jax.ShapeDtyp...  62.5 us
    unnamed x2, local copies, waits for them, and re-layouts  1.46 us

profile of v4, /device:TPU:1, one launch (start us, length us, event | category | flops | bytes accessed | tf_op | source)
XLA Modules:
  0.0 64.6 jit_solution(10864773085529509080)
XLA Ops:
  0.6 62.5 %shard_map.68 = (bf16[48,256]{1,0:T(8,128)(2,1)S(1)}, bf16[576,192]{1,0:T(8,128)(2,1)S(1)}) custom-call(s32[8,48]{1,0:T(8,128)} %bitcast.10, f32[8,48]{1,0:T(8,128)} %bitcast.11, bf16[48,256]{1,0:T(8,128)(2,1)} %grad_hbm.1, bf16[192,576]{1,0:T(8,128)(2,1)} %bitcast.9, bf16[8,2,192,256]{3,2,1,0:T(8,128)(2,1)} %bitcast.8), custom_call_target="tpu_custom_call" | custom-call | tf_op jit(solution)/shard_map/pallas_call | solution.py:442
  63.1 0.9 %copy.7 = bf16[1,576,192]{1,2,0:T(8,128)(2,1)} copy(bf16[1,576,192]{2,1,0:T(8,128)(2,1)S(1)} %bitcast.7) | data formatting | bytes 442368
  64.0 0.6 copy.9
